TPU v7x, 128 devices: a whole 4x4x4 slice. The times are simulated.
128 devices in a mesh: seq: 16 (over z, y), exp: 8 (over x, core).
Axes of the slice: x: 4, y: 4, z: 4, core: 2. Of those that a mesh axis runs over, the one named last changes fastest.
Arguments:
- hidden_in: bfloat16 [2048, 6144], P(('seq', 'exp')), may hold values from -6 to 6
- queries: bfloat16 [2048, 8192], P('seq', 'exp'), may hold values from -4 to 4
- key_rows: bfloat16 [2048, 8192], P('seq', 'exp'), may hold values from -4 to 4
- value_rows: bfloat16 [2048, 8192], P('seq', 'exp'), may hold values from -6 to 6
- out_gate: bfloat16 [2048, 8192], P('seq', 'exp'), may hold values from -6 to 6
- log_decay: float32 [64, 2048], P('exp', 'seq'), may hold values from -1 to 0
- attn_gain: float32 [8192], P('exp'), may hold values from 0.25 to 1.75
- out_weight: bfloat16 [8192, 6144], P('exp'), may hold values from -0.0625 to 0.0625
- ffn_gain: float32 [6144], replicated, may hold values from 0.25 to 1.75
- routes: int32 [2048, 2], P(('seq', 'exp')), may hold values from 0 to 7, all different within a row; in each aligned block of 16 rows (0 to 15, 16 to 31, ...) at most 8 rows name the same one
- combine_weight: float32 [2048, 2], P(('seq', 'exp')), may hold values from 0.2 to 1
- gate_weight: bfloat16 [8, 6144, 4608], P('exp', None, 'seq'), may hold values from -0.078125 to 0.078125
- up_weight: bfloat16 [8, 6144, 4608], P('exp', None, 'seq'), may hold values from -0.078125 to 0.078125
- down_weight: bfloat16 [8, 4608, 6144], P('exp', 'seq'), may hold values from -0.09375 to 0.09375
Outputs:
- layer_out: bfloat16 [2048, 6144], P(('seq', 'exp'))
Inputs may be any that keep to these rules, and one draw needn't show every extreme that they name: `routes`: the two experts of a token differ; in each aligned block of 16 tokens no expert is named more than 8 times, and this most is reached.
All inputs are finite; a program needn't handle non-finite values.
Results may differ from a plain program's by a relative error of at most 0.023.
Values may be sent and summed in bfloat16 or wider, within the bound.
No kernel may reach another device: no remote copies, remote signals or barrier semaphores. Data moves between devices by JAX's collectives and lax.ppermute only.
A program may use at most 128 MiB of HBM per device.

v0:
```python
import jax
import jax.numpy as jnp
from jax import lax
from jax.sharding import PartitionSpec as P


def prefix(value, axis, combine, identity):
    length, here = (lax.axis_size(axis), lax.axis_index(axis))
    everything = jax.tree.map(
        lambda part, kind: lax.all_gather(part.astype(kind), axis),
        value,
        (jnp.bfloat16, jnp.bfloat16),
    )
    start = jax.tree.map(
        lambda part, zero: jnp.broadcast_to(jnp.asarray(zero, part.dtype), part.shape),
        value,
        identity,
    )

    def hop(k, before):
        reached = k < here
        new = combine(
            before, jax.tree.map(lambda part, own: part[k].astype(own.dtype), everything, value)
        )
        return jax.tree.map(lambda a, b: jnp.where(reached, a, b), new, before)

    return lax.fori_loop(0, length, hop, start)


def join_states(earlier, later):
    return (earlier[0] * later[0], later[0][:, None, None] * earlier[1] + later[1])


def per_device(
    hidden_in,
    queries,
    key_rows,
    value_rows,
    out_gate,
    log_decay,
    attn_gain,
    out_weight,
    ffn_gain,
    routes,
    combine_weight,
    gate_weight,
    up_weight,
    down_weight,
):
    f32 = jnp.float32
    block_len = queries.shape[0]
    local_heads = log_decay.shape[0]
    head_size = queries.shape[1] // local_heads
    width = hidden_in.shape[1]
    tok_count = hidden_in.shape[0]
    q_heads = queries.reshape(block_len, local_heads, head_size)
    k_heads = key_rows.reshape(block_len, local_heads, head_size)
    v_heads = value_rows.reshape(block_len, local_heads, head_size)
    cum = jnp.cumsum(log_decay, axis=1)
    ends = cum[:, -1]
    scores = jnp.einsum("thd,shd->hts", q_heads, k_heads, preferred_element_type=f32)
    causal = jnp.arange(block_len)[:, None] >= jnp.arange(block_len)[None, :]
    spread = cum[:, :, None] - cum[:, None, :]
    weights = jnp.where(causal, scores * jnp.exp(jnp.where(causal, spread, 0.0)), 0.0).astype(
        jnp.bfloat16
    )
    intra = jnp.einsum("hts,shd->thd", weights, v_heads, preferred_element_type=f32)
    factor = jnp.exp(ends[None, :] - cum.T)
    keyed = (k_heads.astype(f32) * factor[:, :, None]).astype(jnp.bfloat16)
    state = jnp.einsum("shd,she->hde", keyed, v_heads, preferred_element_type=f32)
    identity = (jnp.ones((local_heads,), f32), jnp.zeros_like(state))
    scanned = prefix((jnp.exp(ends), state), "seq", join_states, identity)
    incoming = scanned[1]
    scaled_q = q_heads.astype(f32) * jnp.exp(cum.T)[:, :, None]
    inter = jnp.einsum("thd,hde->the", scaled_q, incoming, precision=lax.Precision.HIGHEST)
    mixed_heads = intra + inter
    normal_heads = mixed_heads * lax.rsqrt(
        jnp.mean(mixed_heads * mixed_heads, axis=-1, keepdims=True) + 1e-05
    )
    gate_heads = jax.nn.sigmoid(out_gate.reshape(block_len, local_heads, head_size).astype(f32))
    gated = (normal_heads * attn_gain.reshape(local_heads, head_size) * gate_heads).astype(
        jnp.bfloat16
    )
    gated = gated.reshape(block_len, local_heads * head_size)
    mixed = lax.psum_scatter(
        jnp.dot(gated, out_weight, preferred_element_type=f32).astype(jnp.bfloat16),
        "exp",
        scatter_dimension=0,
        tiled=True,
    ).astype(jnp.float32)
    mid_f = (hidden_in.astype(f32) + mixed).astype(jnp.bfloat16).astype(f32)
    normed = (
        mid_f * lax.rsqrt(jnp.mean(mid_f * mid_f, axis=-1, keepdims=True) + 1e-06) * ffn_gain
    ).astype(jnp.bfloat16)
    experts = lax.axis_size("exp")
    capacity = 4 * tok_count // experts
    flat = routes.reshape(-1)
    onehot = (flat[:, None] == jnp.arange(experts, dtype=jnp.int32)[None, :]).astype(jnp.int32)
    earlier = jnp.cumsum(onehot, axis=0) - onehot
    slot = jnp.sum(earlier * onehot, axis=1)
    target = flat * capacity + slot
    placing = (target[None, :] == jnp.arange(experts * capacity, dtype=jnp.int32)[:, None]).astype(
        jnp.bfloat16
    )
    pair_rows = jnp.repeat(normed, 2, axis=0)
    outgoing = (
        jnp.dot(placing, pair_rows, preferred_element_type=f32)
        .astype(jnp.bfloat16)
        .reshape(experts, capacity, width)
    )
    arrived = lax.all_to_all(outgoing, "exp", split_axis=0, concat_axis=0, tiled=True)
    all_rows = lax.all_gather(arrived, "seq", axis=0, tiled=True)
    flat_rows = all_rows.reshape(-1, width)
    w_gate = gate_weight[0]
    w_up = up_weight[0]
    w_down = down_weight[0]
    gate_part = jnp.dot(flat_rows, w_gate, preferred_element_type=f32)
    up_part = jnp.dot(flat_rows, w_up, preferred_element_type=f32)
    hidden = (jax.nn.silu(gate_part) * up_part).astype(jnp.bfloat16)
    summed = lax.psum_scatter(
        jnp.dot(hidden, w_down, preferred_element_type=f32).astype(jnp.bfloat16),
        "seq",
        scatter_dimension=0,
        tiled=True,
    )
    expert_out = summed.reshape(experts, capacity, width)
    returned = lax.all_to_all(expert_out, "exp", split_axis=0, concat_axis=0, tiled=True)
    picked = jnp.dot(placing.T, returned.reshape(-1, width), preferred_element_type=f32)
    weighted = jnp.sum(picked.reshape(tok_count, 2, width) * combine_weight[:, :, None], axis=1)
    return (mid_f + weighted).astype(jnp.bfloat16)


def solution(mesh):
    return jax.shard_map(
        per_device,
        mesh=mesh,
        in_specs=(
            P(("seq", "exp"), None),
            P("seq", "exp"),
            P("seq", "exp"),
            P("seq", "exp"),
            P("seq", "exp"),
            P("exp", "seq"),
            P("exp"),
            P("exp", None),
            P(),
            P(("seq", "exp"), None),
            P(("seq", "exp"), None),
            P("exp", None, "seq"),
            P("exp", None, "seq"),
            P("exp", "seq", None),
        ),
        out_specs=P(("seq", "exp"), None),
        check_vma=False,
    )
```

profile of v0, /device:TPU:16, one launch (start us, length us, event | category | flops | bytes accessed | tf_op | source)
XLA Modules:
  0.0 414.4 jit_solution(11902706022788605641)
XLA Ops:
  6.5 1.1 reduce_window_sum.22
  7.9 1.8 copy.58
  9.7 2.0 convolution_convert_fusion.3
  11.8 1.2 dynamic-slice
  14.1 37.6 %all-reduce = bf16[128]{0:T(256)(128)(2,1)S(1)} all-reduce(bf16[128]{0:T(256)(128)(2,1)S(1)} %dynamic-update-slice), channel_id=2, replica_groups=mesh['seq'=16,'exp'=8] {'seq'}, use_global_device_ids=true, to_apply=%add | all-reduce | flops 128 | bytes 512
  52.4 1.9 add_divide_fusion
  54.4 2.0 copy.54
  57.0 8.8 %all-gather.7.cloned.1.call-done = bf16[128,128,128]{2,1,0:T(8,128)(2,1)} async-done(((bf16[8,128,128]{2,1,0:T(8,128)(2,1)}), bf16[128,128,128]{2,1,0:T(8,128)(2,1)}) %all-gather.7.cloned.1.call-update) | async-done | bytes 4194320 | tf_op jit(solution)/shard_map/all_gather | solution.py:10
  65.8 43.8 %while.14 = (s32[]{:T(128)}, f32[8,128,128]{2,1,0:T(8,128)}, s32[]{:T(128)}, bf16[16,8]{1,0:T(8,128)(2,1)}, bf16[16,8,128,128]{3,2,1,0:T(8,128)(2,1)}, /*index=5*/s32[]{:T(128)}, s32[]{:T(128)}) while((s32[]{:T(128)}, f32[8,128,128]{2,1,0:T(8,128)}, s32[]{:T(128)}, bf16[16,8]{1,0:T(8,128)(2,1)}, ...), condition=%wide.region_2.3_spmd.clone, body=%wide.region_1.2_spmd.clone.sunk | while | flops 655372 | bytes 1310905 | solution.py:27
  66.5 1.9 fusion.69
  69.1 2.1 fusion.69
  71.8 2.1 fusion.69
  74.6 2.1 fusion.69
  77.3 2.1 fusion.69
  80.1 2.1 fusion.69
  82.8 2.1 fusion.69
  85.6 2.1 fusion.69
  88.3 2.1 fusion.69
  91.1 2.1 fusion.69
  93.8 2.1 fusion.69
  96.6 2.1 fusion.69
  99.3 2.1 fusion.69
  102.1 2.1 fusion.69
  104.8 2.1 fusion.69
  107.6 2.1 fusion.69
  109.7 3.1 convolution_bitcast_fusion.1
  112.8 2.6 multiply_reduce_fusion
  115.4 1.4 multiply_convert_fusion
  116.8 7.6 %convolution_convert_fusion.1 = bf16[128,6144]{1,0:T(8,128)(2,1)} fusion(bf16[128,1024]{0,1:T(8,128)(2,1)S(1)} %bitcast.98, bf16[1024,6144]{1,0:T(8,128)(2,1)} %param.23), kind=kOutput, calls=%fused_computation.8 | convolution fusion | flops 1611399168 | bytes 14417920 | tf_op jit(solution)/shard_map/dot_general | solution.py:86
  126.7 0.8 select_reduce_fusion
  128.6 28.2 %reduce-scatter.3.cloned.1.call-done = bf16[16,6144]{1,0:T(8,128)(2,1)} async-done(((bf16[128,6144]{1,0:T(8,128)(2,1)}), bf16[16,6144]{1,0:T(8,128)(2,1)}) %reduce-scatter.3.cloned.1.call-update) | async-done | bytes 196624 | tf_op jit(solution)/shard_map/reduce_scatter | solution.py:85
  156.8 1.2 fusion.29
  158.1 1.1 fusion.31
  159.2 1.0 broadcast_in_dim.19
  160.2 1.9 reshape.119
  162.1 1.3 fusion.5
  163.4 16.3 %all_to_all.10 = bf16[8,8,6144]{2,1,0:T(8,128)(2,1)} all-to-all(bf16[8,8,6144]{2,1,0:T(8,128)(2,1)S(1)} %fusion.5), channel_id=1, replica_groups=mesh['seq'=16,'exp'=8] {'exp'}, dimensions={0} | all-to-all | bytes 1572864 | tf_op jit(solution)/shard_map/all_to_all | solution.py:111
  180.0 89.4 %all-gather.5.cloned.1.call-done = bf16[128,8,6144]{2,1,0:T(8,128)(2,1)} async-done(((bf16[8,8,6144]{2,1,0:T(8,128)(2,1)}), bf16[128,8,6144]{2,1,0:T(8,128)(2,1)}) %all-gather.5.cloned.1.call-update) | async-done | bytes 12582928 | tf_op jit(solution)/shard_map/all_gather | solution.py:112
  269.4 8.2 %fusion.3 = f32[1024,288]{0,1:T(8,128)S(1)} fusion(bf16[128,8,6144]{2,1,0:T(8,128)(2,1)} %all-gather.5.cloned.1.call-done, bf16[1,6144,288]{1,2,0:T(8,128)(2,1)} %param.27), kind=kOutput, calls=%fused_computation.5 | convolution fusion | flops 3623878656 | bytes 17301504 | tf_op jit(solution)/shard_map/dot_general | solution.py:117
  277.6 1.0 copy-done.7
  278.6 1.0 copy-done.8
  279.6 4.0 fusion.14
  283.6 9.7 %convolution_convert_fusion = bf16[1024,6144]{1,0:T(8,128)(2,1)} fusion(bf16[1024,288]{0,1:T(8,128)(2,1)S(1)} %fusion.14, bf16[1,288,6144]{2,1,0:T(8,128)(2,1)S(1)} %copy-done), kind=kOutput, calls=%fused_computation.7 | convolution fusion | flops 3630170112 | bytes 16711680 | tf_op jit(solution)/shard_map/dot_general | solution.py:121
  293.3 93.7 %reduce-scatter.5.cloned.1.call-done = bf16[64,6144]{1,0:T(8,128)(2,1)} async-done(((bf16[1024,6144]{1,0:T(8,128)(2,1)}), bf16[64,6144]{1,0:T(8,128)(2,1)}) %reduce-scatter.5.cloned.1.call-update) | async-done | bytes 786448 | tf_op jit(solution)/shard_map/reduce_scatter | solution.py:120
  387.0 4.3 %all-to-all-start.1 = ((bf16[8,8,6144]{2,1,0:T(8,128)(2,1)}), bf16[8,8,6144]{2,1,0:T(8,128)(2,1)}, u32[]{:S(2)}, u32[]{:S(2)}) async-start(bf16[8,8,6144]{2,1,0:T(8,128)(2,1)} %bitcast.101), calls=%async_computation.3 | async-start | bytes 1572864 | tf_op jit(solution)/shard_map/all_to_all | solution.py:127
  391.5 13.1 %all-to-all-done.1 = bf16[8,8,6144]{2,1,0:T(8,128)(2,1)} async-done(((bf16[8,8,6144]{2,1,0:T(8,128)(2,1)}), bf16[8,8,6144]{2,1,0:T(8,128)(2,1)}, u32[]{:S(2)}, u32[]{:S(2)}) %all-to-all-start.1) | async-done | bytes 786464 | tf_op jit(solution)/shard_map/all_to_all | solution.py:127
  404.6 1.5 fusion.19
  406.1 1.8 fusion.32
  (58 shorter events, 16.9 us)
Async XLA Ops:
  6.5 277.1 %copy-start = (bf16[1,288,6144]{2,1,0:T(8,128)(2,1)S(1)}, bf16[1,288,6144]{2,1,0:T(8,128)(2,1)}, u32[]{:S(2)}) copy-start(bf16[1,288,6144]{2,1,0:T(8,128)(2,1)} %param.29) | copy-start | bytes 10616836
  6.5 59.3 %all-gather.7.cloned.1.call-start = ((), (), s32[]{:S(2)}) async-start(), calls=%async_computation.7 | async-start | bytes 4456448 | tf_op jit(solution)/shard_map/all_gather | solution.py:10
  11.7 145.1 %reduce-scatter.3.cloned.1.call-start = ((), (), s32[]{:S(2)}) async-start(), calls=%async_computation.4 | async-start | bytes 1769472 | tf_op jit(solution)/shard_map/reduce_scatter | solution.py:85
  65.8 49.6 %copy-start.2 = (f32[1024]{0:T(1024)S(1)}, f32[1024]{0:T(1024)}, u32[]{:S(2)}) copy-start(f32[1024]{0:T(1024)} %param.22) | copy-start | bytes 12292
  116.8 7.7 %copy-start.3 = (s32[16,2]{0,1:T(2,128)S(1)}, s32[16,2]{0,1:T(2,128)}, u32[]{:S(2)}) copy-start(s32[16,2]{0,1:T(2,128)} %param.25) | copy-start | bytes 388
  124.4 145.0 %all-gather.5.cloned.1.call-start = ((), (), s32[]{:S(2)}) async-start(), calls=%async_computation.5 | async-start | bytes 13369344 | tf_op jit(solution)/shard_map/all_gather | solution.py:112
  124.7 0.5 copy-start.1
  127.5 0.5 copy-start.5
  179.8 207.3 %reduce-scatter.5.cloned.1.call-start = ((), (), s32[]{:S(2)}) async-start(), calls=%async_computation.6 | async-start | bytes 13369344 | tf_op jit(solution)/shard_map/reduce_scatter | solution.py:120
  269.4 9.2 %copy-start.7 = (bf16[128,8,6144]{2,1,0:T(8,128)(2,1)S(1)}, bf16[128,8,6144]{2,1,0:T(8,128)(2,1)}, u32[]{:S(2)}) copy-start(bf16[128,8,6144]{2,1,0:T(8,128)(2,1)} %all-gather.5.cloned.1.call-done) | copy-start | bytes 37748740
  269.4 10.2 %copy-start.8 = (bf16[1,6144,288]{1,2,0:T(8,128)(2,1)S(1)}, bf16[1,6144,288]{1,2,0:T(8,128)(2,1)}, u32[]{:S(2)}) copy-start(bf16[1,6144,288]{1,2,0:T(8,128)(2,1)} %param.28) | copy-start | bytes 10616836
  293.3 98.0 %copy-start.6 = (s32[32]{0:T(128)S(1)}, s32[32]{0:T(128)}, u32[]{:S(2)}) copy-start(s32[32]{0:T(128)} %copy-done.5) | copy-start | bytes 388
  293.3 98.2 %copy-start.4 = (s32[16,2]{0,1:T(2,128)S(1)}, s32[16,2]{0,1:T(2,128)}, u32[]{:S(2)}) copy-start(s32[16,2]{0,1:T(2,128)} %param.25) | copy-start | bytes 388
  387.0 17.5 %all-to-all-start.1 = ((bf16[8,8,6144]{2,1,0:T(8,128)(2,1)}), bf16[8,8,6144]{2,1,0:T(8,128)(2,1)}, u32[]{:S(2)}, u32[]{:S(2)}) async-start(bf16[8,8,6144]{2,1,0:T(8,128)(2,1)} %bitcast.101), calls=%async_computation.3 | async-start | bytes 1572864 | tf_op jit(solution)/shard_map/all_to_all | solution.py:127
Sparse Core Ops, SparseCore 0:
  11.8 53.9 all-gather.6
  124.6 32.2 reduce-scatter.2
  179.9 89.5 all-gather.4
  293.4 93.5 reduce-scatter.4
where the time goes:
time: 417 us; the launch traced here: 414 us
  waiting for transfers between devices  233 us (56%)
  other arithmetic  56.2 us (13%)
  blocking collectives  54 us (13%)
  matrix products  39.9 us (10%)
  between operations  13.9 us (3%)
  local copies, waits for them, and re-layouts  12.5 us (3%)
  starting transfers between devices  4.59 us (1%)
    reduce_scatter x1, waiting for transfers between devices, per_device(): lax.psum_scatter(jnp.dot(hidden, w_down, preferred_element_type=f32).asty...  93.7 us
    all_gather x1, waiting for transfers between devices, per_device(): all_rows = lax.all_gather(arrived, 'seq', axis=0, tiled=True)  89.4 us
    unnamed x1, blocking collectives  37.6 us
    select_n x16, other arithmetic, hop(): return jax.tree.map(lambda a, b: jnp.where(reached, a, b), new, before)  32.9 us
    reduce_scatter x1, waiting for transfers between devices, per_device(): lax.psum_scatter(jnp.dot(gated, out_weight, preferred_element_type=f32).a...  28.2 us
    all_to_all x1, blocking collectives, per_device(): lax.all_to_all(outgoing, 'exp', split_axis=0, concat_axis=0, tiled=True)  16.3 us
    all_to_all x1, waiting for transfers between devices, per_device(): lax.all_to_all(expert_out, 'exp', split_axis=0, concat_axis=0, tiled=True)  13.1 us
    convert_element_type x16, other arithmetic, hop(): part[k].astype(own.dtype)  11 us
  transfers between devices with their start and end apart: 5, of which 5 were waited for; matrix products, arithmetic and copies ran while one was open for 2% of the time, Pallas kernels for 0%

commit v1 on v0

v1 whole, which is shorter than its diff:
```python
import functools

import jax
import jax.numpy as jnp
from jax import lax
from jax.experimental import pallas as pl
from jax.experimental.pallas import tpu as pltpu
from jax.sharding import PartitionSpec as P

f32 = jnp.float32
bf16 = jnp.bfloat16
SIDE = 4
CORES = 2
AXES = ("seq", "exp")
HD = 128
VMEM_LIMIT = 48 * 1024 * 1024


def permutation(move):
    pairs = []
    for z in range(SIDE):
        for y in range(SIDE):
            for x in range(SIDE):
                for c in range(CORES):
                    z2, y2, x2, c2 = move(z, y, x, c)
                    source = ((z * SIDE + y) * SIDE + x) * CORES + c
                    target = (((z2 % SIDE) * SIDE + y2 % SIDE) * SIDE + x2 % SIDE) * CORES + c2
                    pairs.append((source, target))
    return pairs


def along_x(k):
    return permutation(lambda z, y, x, c: (z, y, x + k, c))


def along_first(k):
    return permutation(lambda z, y, x, c: (z, y + k, x, c) if c == 0 else (z + k, y, x, c))


def along_second(k):
    return permutation(lambda z, y, x, c: (z + k, y, x, c) if c == 0 else (z, y + k, x, c))


OTHER_CORE = permutation(lambda z, y, x, c: (z, y, x, 1 - c))


def send(value, perm):
    return lax.ppermute(value, AXES, perm)


def split3(value):
    high = lax.reduce_precision(value, 8, 7)
    rest = value - high
    mid = lax.reduce_precision(rest, 8, 7)
    return high, mid, rest - mid


def lower_triangle(n):
    row = lax.broadcasted_iota(jnp.int32, (n, n), 0)
    col = lax.broadcasted_iota(jnp.int32, (n, n), 1)
    return row >= col


def dot_nt(a, b, **kw):
    return lax.dot_general(a, b, (((1,), (1,)), ((), ())), preferred_element_type=f32, **kw)


def dot_tn(a, b, **kw):
    return lax.dot_general(a, b, (((0,), (0,)), ((), ())), preferred_element_type=f32, **kw)


def state_kernel(k_ref, v_ref, ld_ref, out_ref):
    heads, block = ld_ref.shape
    low = lower_triangle(block).astype(f32)
    ld = ld_ref[...]
    cum_col = dot_nt(low, ld, precision=lax.Precision.HIGHEST)
    ends = cum_col[block - 1 : block, :]
    factor = jnp.exp(ends - cum_col)
    rows = lax.broadcasted_iota(jnp.int32, (16, HD), 0)
    for h in range(heads):
        lanes = pl.ds(h * HD, HD)
        keyed = (k_ref[:, lanes].astype(f32) * factor[:, h : h + 1]).astype(bf16)
        state = dot_tn(keyed, v_ref[:, lanes]).astype(bf16)
        end = jnp.broadcast_to(ends[:, h : h + 1], (16, HD))
        high = end.astype(bf16).astype(f32)
        rest = end - high
        mid = rest.astype(bf16).astype(f32)
        tail = jnp.where(rows == 0, high, jnp.where(rows == 1, mid, jnp.where(rows == 2, rest - mid, 0.0)))
        tail = tail.astype(bf16)
        for part in range(2):
            out_ref[2 * h + part, 0:64, :] = state[part * 64 : part * 64 + 64]
            out_ref[2 * h + part, 64:80, :] = tail


def scan_kernel(in_ref, out_ref):
    count = in_ref.shape[0]
    carry = jnp.zeros((64, HD), f32)
    for i in range(count):
        out_ref[i] = carry.astype(bf16)
        if i + 1 < count:
            tail = in_ref[i, 64:80, :].astype(f32)
            end = tail[0:1] + tail[1:2] + tail[2:3]
            carry = jnp.exp(end) * carry + in_ref[i, 0:64, :].astype(f32)


def mix_kernel(place, q_ref, k_ref, v_ref, g_ref, ld_ref, inc_ref, gain_ref, w_ref, out_ref, gated):
    heads, block = ld_ref.shape
    core = place[1]

    @pl.when(pl.program_id(0) == 0)
    def _():
        causal = lower_triangle(block)
        low = causal.astype(f32)
        ld = ld_ref[...]
        cum_col = dot_nt(low, ld, precision=lax.Precision.HIGHEST)
        cum_row = dot_nt(ld, low, precision=lax.Precision.HIGHEST)
        grown = jnp.exp(cum_col)
        for h in range(heads):
            lanes = pl.ds(h * HD, HD)
            q, k, v = q_ref[:, lanes], k_ref[:, lanes], v_ref[:, lanes]
            spread = cum_col[:, h : h + 1] - cum_row[h : h + 1, :]
            weights = jnp.where(causal, dot_nt(q, k) * jnp.exp(jnp.where(causal, spread, 0.0)), 0.0)
            intra = jnp.dot(weights.astype(bf16), v, preferred_element_type=f32)
            inter = jnp.dot(q, inc_ref[h], preferred_element_type=f32) * grown[:, h : h + 1]
            mixed = intra + inter
            normal = mixed * lax.rsqrt(jnp.mean(mixed * mixed, axis=-1, keepdims=True) + 1e-05)
            gate = 1.0 / (1.0 + jnp.exp(-g_ref[:, lanes].astype(f32)))
            result = (normal * gain_ref[:, lanes] * gate).astype(bf16)
            for x in range(SIDE):
                for c in range(CORES):
                    there, here = c * 64 + x * 16, x * 32 + c * 16
                    gated[there : there + 16, lanes] = result[here : here + 16]

    product = jnp.dot(gated[...], w_ref[...], preferred_element_type=f32).astype(bf16)
    out_ref[core, 0] = product[:64]
    out_ref[1 - core, 0] = product[64:]


def attention(place, queries, key_rows, value_rows, out_gate, log_decay, attn_gain, out_weight):
    heads = log_decay.shape[0]
    block = queries.shape[0]
    width = out_weight.shape[1]
    pieces = pl.pallas_call(
        state_kernel,
        out_shape=jax.ShapeDtypeStruct((2 * heads, 80, HD), bf16),
        compiler_params=pltpu.CompilerParams(vmem_limit_bytes=VMEM_LIMIT),
    )(key_rows, value_rows, log_decay)
    pieces = lax.all_to_all(pieces, "seq", split_axis=0, concat_axis=0, tiled=True)
    before = pl.pallas_call(
        scan_kernel,
        out_shape=jax.ShapeDtypeStruct((2 * heads, 64, HD), bf16),
        compiler_params=pltpu.CompilerParams(vmem_limit_bytes=VMEM_LIMIT),
    )(pieces)
    before = lax.all_to_all(before, "seq", split_axis=0, concat_axis=0, tiled=True)
    incoming = before.reshape(heads, HD, HD)
    tile = 512
    per = width // SIDE // tile
    whole = lambda *shape: pl.BlockSpec(shape, lambda j, p: (0,) * len(shape))
    return pl.pallas_call(
        mix_kernel,
        grid_spec=pltpu.PrefetchScalarGridSpec(
            num_scalar_prefetch=1,
            grid=(width // tile,),
            in_specs=[whole(block, heads * HD)] * 4
            + [
                whole(heads, block),
                whole(heads, HD, HD),
                whole(1, heads * HD),
                pl.BlockSpec((heads * HD, tile), lambda j, p: (0, j)),
            ],
            out_specs=pl.BlockSpec(
                (2, 1, 64, tile), lambda j, p: (0, lax.rem(j // per + SIDE - p[0], SIDE), 0, lax.rem(j, per))
            ),
            scratch_shapes=[pltpu.VMEM((block, heads * HD), bf16)],
        ),
        out_shape=jax.ShapeDtypeStruct((CORES, SIDE, 64, width // SIDE), bf16),
        compiler_params=pltpu.CompilerParams(vmem_limit_bytes=VMEM_LIMIT),
    )(place, queries, key_rows, value_rows, out_gate, log_decay, incoming, attn_gain.reshape(1, -1), out_weight)


def gate_up_kernel(groups, ids, *refs):
    x_refs, (own_ref, swap_ref, out_ref, acc) = refs[:-4], refs[-4:]
    step = pl.program_id(0)
    depth = own_ref.shape[2]
    wide = own_ref.shape[1]
    blocks = [(ref, i) for ref in x_refs for i in range(ref.shape[0])]
    rows = len(blocks) * 64
    x = jnp.concatenate([ref[...].reshape(-1, ref.shape[2])[:, :depth] for ref in x_refs], 0)
    meta = jnp.concatenate([ref[...].reshape(-1, ref.shape[2])[:, depth:] for ref in x_refs], 0)
    first = meta[:, 64:65].astype(f32)
    second = meta[:, 65:66].astype(f32)
    for which, w_ref in ((0, own_ref), (1, swap_ref)):
        expert = ids[2 + which * 4 + step].astype(f32)
        part = dot_nt(x, w_ref[0])
        acc[0, :, :wide] = jnp.where(first == expert, part, acc[0, :, :wide])
        acc[1, :, :wide] = jnp.where(second == expert, part, acc[1, :, :wide])

    @pl.when(step == pl.num_programs(0) - 1)
    def _():
        lane = lax.broadcasted_iota(jnp.int32, (rows, 128), 1)
        edge = wide // 128 * 128
        for k in range(2):
            last = jnp.where(lane < 64, acc[k, :, edge : edge + 128], meta.astype(f32)).astype(bf16)
            head = acc[k, :, :edge].astype(bf16)
            for i in range(len(blocks)):
                rel = lax.rem(i % 4 + SIDE - ids[0], SIDE)
                at = k * (edge + 128)
                out_ref[rel, i // 4, :, at : at + edge] = head[i * 64 : i * 64 + 64]
                out_ref[rel, i // 4, :, at + edge : at + edge + 128] = last[i * 64 : i * 64 + 64]


def gate_up(ids, xs, own, swap):
    count = sum(x.shape[0] for x in xs)
    groups = count // SIDE
    wide = own.shape[1]
    padded = wide // 128 * 128 + 128
    whole = lambda shape: pl.BlockSpec(shape, lambda j, p: (0,) * len(shape))
    shape = (SIDE, groups, 64, 2 * padded)
    return pl.pallas_call(
        functools.partial(gate_up_kernel, groups),
        grid_spec=pltpu.PrefetchScalarGridSpec(
            num_scalar_prefetch=1,
            grid=(SIDE,),
            in_specs=[whole(x.shape) for x in xs]
            + [pl.BlockSpec((1,) + own.shape[1:], lambda j, p: (j, 0, 0))] * 2,
            out_specs=whole(shape),
            scratch_shapes=[pltpu.VMEM((2, count * 64, padded), f32)],
        ),
        out_shape=jax.ShapeDtypeStruct(shape, bf16),
        compiler_params=pltpu.CompilerParams(vmem_limit_bytes=VMEM_LIMIT),
    )(ids, *xs, own, swap)


def down_kernel(ids, h_ref, own_ref, swap_ref, out_ref, spread):
    rows = h_ref.shape[1] * 64
    h = h_ref[0].reshape(rows, h_ref.shape[3]).astype(f32)
    pad = own_ref.shape[1]
    first = h[:, 288:289]
    second = h[:, 289:290]
    for which in range(2):
        for j in range(SIDE):
            expert = ids[2 + which * 4 + j].astype(f32)
            kept = jnp.where(first == expert, h[:, :pad], 0.0) + jnp.where(second == expert, h[:, pad:], 0.0)
            spread[:, (which * 4 + j) * pad : (which * 4 + j + 1) * pad] = kept.astype(bf16)
    half = SIDE * pad
    result = jnp.dot(spread[:, :half], own_ref[...].reshape(half, -1), preferred_element_type=f32)
    result += jnp.dot(spread[:, half:], swap_ref[...].reshape(half, -1), preferred_element_type=f32)
    out_ref[...] = result.astype(bf16).reshape(out_ref.shape)


def down(ids, hidden, own, swap):
    width = own.shape[2]
    shape = (SIDE, SIDE, 64, width)
    whole = lambda shape: pl.BlockSpec(shape, lambda j, p: (0,) * len(shape))
    return pl.pallas_call(
        down_kernel,
        grid_spec=pltpu.PrefetchScalarGridSpec(
            num_scalar_prefetch=1,
            grid=(SIDE,),
            in_specs=[
                pl.BlockSpec((1,) + hidden.shape[1:], lambda j, p: (j, 0, 0, 0)),
                whole(own.shape),
                whole(swap.shape),
            ],
            out_specs=pl.BlockSpec((SIDE, 1, 64, width), lambda j, p: (0, p[10 + j], 0, 0)),
            scratch_shapes=[pltpu.VMEM((hidden.shape[1] * 64, 8 * own.shape[1]), bf16)],
        ),
        out_shape=jax.ShapeDtypeStruct(shape, bf16),
        compiler_params=pltpu.CompilerParams(vmem_limit_bytes=VMEM_LIMIT),
    )(ids, hidden, own, swap)


def ring_gather(value, perm):
    half = value.shape[0] // 2
    right = send(value, perm(1))
    left = send(value, perm(-1))
    far = (send(right[:half], perm(1)), send(left[half:], perm(-1)))
    return right, left, far


def plus(a, b):
    return (a.astype(f32) + b.astype(f32)).astype(bf16)


def ring_reduce(own, behind, ahead, far, perm):
    half = far.shape[0] // 2
    from_behind = send(far[:half], perm(1))
    from_ahead = send(far[half:], perm(-1))
    to_ahead = jnp.concatenate([plus(ahead[:half], from_behind), ahead[half:]], 0)
    to_behind = jnp.concatenate([behind[:half], plus(behind[half:], from_ahead)], 0)
    got = send(to_ahead, perm(1)), send(to_behind, perm(-1))
    return own.astype(f32) + got[0].astype(f32) + got[1].astype(f32)


def per_device(
    hidden_in,
    queries,
    key_rows,
    value_rows,
    out_gate,
    log_decay,
    attn_gain,
    out_weight,
    ffn_gain,
    routes,
    combine_weight,
    gate_weight,
    up_weight,
    down_weight,
):
    width = hidden_in.shape[1]
    part = width // SIDE
    units = gate_weight.shape[2]
    at = lax.axis_index("exp")
    x, core = at // CORES, lax.rem(at, CORES)
    order = [0, -1, 1, 2]
    chips = [lax.rem(x + d + SIDE, SIDE) for d in order]
    place = jnp.stack(
        [x, core]
        + [2 * chip + core for chip in chips]
        + [2 * chip + 1 - core for chip in chips]
        + chips
    ).astype(jnp.int32)

    gate_t, up_t, down_w = gate_weight[0].T, up_weight[0].T, down_weight[0]

    def piece(d):
        start = lax.rem(x + d + SIDE, SIDE) * part
        cut = lambda w: lax.dynamic_slice(w, (0, start), (units, part))
        return jnp.concatenate([cut(gate_t), cut(up_t)], 0), cut(down_w)

    mine, ahead, behind, far = piece(0), piece(1), piece(-1), piece(2)
    gu = [mine[0], send(ahead[0], along_x(1)), send(behind[0], along_x(-1)), send(far[0], along_x(2))]
    gu_own = jnp.stack(gu)
    gu_swap = send(gu_own, OTHER_CORE)
    dn = [mine[1], send(ahead[1], along_x(1)), send(behind[1], along_x(-1)), send(far[1], along_x(2))]
    pad = -units % 128
    dn_own = jnp.stack([jnp.pad(d, ((0, pad), (0, 0))) for d in dn])
    dn_swap = send(dn_own, OTHER_CORE)

    toks = hidden_in.shape[0]
    routes_f = routes.astype(f32)
    cw = split3(combine_weight)
    lanes = [routes_f[:, 0:1], routes_f[:, 1:2]] + [w[:, k : k + 1] for k in range(2) for w in cw]
    meta = jnp.concatenate([jnp.zeros((toks, 64), f32)] + lanes + [jnp.zeros((toks, 64 - len(lanes)), f32)], 1)
    stacked = jnp.concatenate(
        [
            hidden_in.reshape(toks, SIDE, part).transpose(1, 0, 2),
            jnp.broadcast_to(meta.astype(bf16)[None], (SIDE, toks, 128)),
        ],
        2,
    )
    groups = [[2 * i + c + 8 * s for i in range(SIDE)] for s in range(16) for c in range(CORES)]
    here = lax.all_to_all(
        stacked, "exp", split_axis=0, concat_axis=0, tiled=True,
        axis_index_groups=[[2 * i + c for i in range(SIDE)] for c in range(CORES)],
    ).reshape(SIDE * toks, part + 128)

    partial = attention(place, queries, key_rows, value_rows, out_gate, log_decay, attn_gain, out_weight)
    summed = plus(partial[0], send(partial[1], OTHER_CORE))
    got = [send(summed[1], along_x(1)), send(summed[3], along_x(-1)), send(summed[2], along_x(2))]
    mixed = summed[0].astype(f32)
    for g in got:
        mixed = mixed + g.astype(f32)
    mid = (here[:, :part].astype(f32) + mixed).astype(bf16)
    mid_f = mid.astype(f32)
    gain = lax.dynamic_slice(ffn_gain, (x * part,), (part,))
    squares = split3(jnp.sum(mid_f * mid_f, axis=1, keepdims=True))
    tail = here[:, part:]
    tail = jnp.concatenate([tail[:, :72], squares[0].astype(bf16), squares[1].astype(bf16), tail[:, 74:]], 1)
    rows = jnp.concatenate([(mid_f * gain).astype(bf16), tail], 1)

    right, left, far = ring_gather(rows, along_first)
    plane = jnp.stack([rows, right, left, jnp.concatenate(far, 0)])
    right, left, far = ring_gather(plane, along_second)
    y_near = gate_up(place, [plane], gu_own, gu_swap)
    y_far = gate_up(place, [right, left, far[0], far[1]], gu_own, gu_swap)
    y = jnp.concatenate([y_near, y_far], 1)
    z = ring_reduce(y[0], y[3], y[1], y[2], along_x)

    wide = 2 * units
    col = z.shape[2] // 2
    scale = lax.rsqrt((z[:, :, wide + 8 : wide + 9] + z[:, :, wide + 9 : wide + 10]) / width + 1e-06)
    hidden = []
    for k in range(2):
        gate = z[:, :, k * col : k * col + units] * scale
        up = z[:, :, k * col + units : k * col + wide] * scale
        lane = wide + 2 + 3 * k
        weight = jnp.sum(z[:, :, lane : lane + 3], axis=2, keepdims=True) * (1.0 / SIDE)
        value = jax.nn.silu(gate) * up * weight
        extra = z[:, :, wide : wide + 2] * (1.0 / SIDE)
        hidden += [value, extra, jnp.zeros(value.shape[:2] + (pad - 2,), f32)]
    hidden = jnp.concatenate(hidden, 2).astype(bf16)
    right, left, far = ring_gather(hidden, along_x)
    hidden = jnp.stack([hidden, right, left, jnp.concatenate(far, 0)])
    out = down(place, hidden, dn_own, dn_swap)
    out = ring_reduce(out[0], out[1], out[2], out[3], along_second).astype(bf16)
    out = ring_reduce(out[0], out[1], out[2], out[3], along_first)
    out = (mid_f + out).astype(bf16).reshape(SIDE, toks, part)
    out = lax.all_to_all(
        out, "exp", split_axis=0, concat_axis=0, tiled=True,
        axis_index_groups=[[2 * i + c for i in range(SIDE)] for c in range(CORES)],
    )
    return out.transpose(1, 0, 2).reshape(toks, width)


def solution(mesh):
    return jax.shard_map(
        per_device,
        mesh=mesh,
        in_specs=(
            P(("seq", "exp"), None),
            P("seq", "exp"),
            P("seq", "exp"),
            P("seq", "exp"),
            P("seq", "exp"),
            P("exp", "seq"),
            P("exp"),
            P("exp", None),
            P(),
            P(("seq", "exp"), None),
            P(("seq", "exp"), None),
            P("exp", None, "seq"),
            P("exp", None, "seq"),
            P("exp", "seq", None),
        ),
        out_specs=P(("seq", "exp"), None),
        check_vma=False,
    )
```

time: 417 us -> 352 us (0.84)
  starting transfers between devices: 4.59 us -> 82.7 us
  waiting for transfers between devices: 233 us -> 161 us
  Pallas kernels: 0 us -> 57.3 us
  other arithmetic: 56.2 us -> 12.9 us
  matrix products: 39.9 us -> 0 us
  blocking collectives: 54 us -> 26.7 us
  between operations: 13.9 us -> 0.6 us
    ppermute x0 -> x36, waiting for transfers between devices: none -> 154 us  [send(): return lax.ppermute(value, AXES, perm)]
    reduce_scatter x2 -> x0, waiting for transfers between devices: 122 us -> none  [the longest x1 93.7 us: per_device(): lax.psum_scatter(jnp.dot(hidden, w_down, preferred_element_type=f32).asty...]
    all_gather x2 -> x0, waiting for transfers between devices: 98.2 us -> none  [the longest x1 89.4 us: per_device(): all_rows = lax.all_gather(arrived, 'seq', axis=0, tiled=True)]
    ppermute x0 -> x36, starting transfers between devices: none -> 73.3 us  [send(): return lax.ppermute(value, AXES, perm)]
    pallas_call x0 -> x6, Pallas kernels: none -> 57.3 us  [the longest x2 28.4 us: gate_up(): pl.pallas_call(functools.partial(gate_up_kernel, groups), grid_spec=pltpu...]
    dot_general x9 -> x0, matrix products: 39.9 us -> none  [the longest x1 9.66 us: per_device(): jnp.dot(hidden, w_down, preferred_element_type=f32).astype(jnp.bfloat16)]
    unnamed x1 -> x0, blocking collectives: 37.6 us -> none
    select_n x16 -> x0, other arithmetic: 32.9 us -> none  [hop(): return jax.tree.map(lambda a, b: jnp.where(reached, a, b), new, before)]
  transfers between devices with their start and end apart: 5 -> 38, of which waited for: 5 -> 20; matrix products, arithmetic and copies ran while one was open for 2% -> 4% of each run, Pallas kernels for 0% -> 12%
where the time goes in v1:
time: 352 us
  waiting for transfers between devices  161 us (46%)
  starting transfers between devices  82.7 us (23%)
  Pallas kernels  57.3 us (16%)
  blocking collectives  26.7 us (8%)
  other arithmetic  12.9 us (4%)
  local copies, waits for them, and re-layouts  11 us (3%)
    ppermute x36, waiting for transfers between devices, send(): return lax.ppermute(value, AXES, perm)  154 us
    ppermute x36, starting transfers between devices, send(): return lax.ppermute(value, AXES, perm)  73.3 us
    pallas_call x2, Pallas kernels, gate_up(): pl.pallas_call(functools.partial(gate_up_kernel, groups), grid_spec=pltpu...  28.4 us
    pallas_call x1, Pallas kernels, down(): pl.pallas_call(down_kernel, grid_spec=pltpu.PrefetchScalarGridSpec(num_sc...  15.6 us
    all_to_all x1, blocking collectives, attention(): lax.all_to_all(pieces, 'seq', split_axis=0, concat_axis=0, tiled=True)  15.5 us
    pallas_call x1, Pallas kernels, attention(): pl.pallas_call(mix_kernel, grid_spec=pltpu.PrefetchScalarGridSpec(num_sca...  11.8 us
    all_to_all x1, blocking collectives, per_device(): lax.all_to_all(out, 'exp', split_axis=0, concat_axis=0, tiled=True, axis_...  11.2 us
  transfers between devices with their start and end apart: 38, of which 20 were waited for; matrix products, arithmetic and copies ran while one was open for 4% of the time, Pallas kernels for 12%

profile of v1, /device:TPU:16, one launch (start us, length us, event | category | flops | bytes accessed | tf_op | source)
XLA Modules:
  0.0 351.8 jit_solution(17109095026162665931)
XLA Ops:
  0.0 3.5 dynamic-slice_bitcast_fusion.10
  3.6 1.6 collective-permute-start.8
  5.3 1.8 collective-permute-start.9
  7.2 1.9 collective-permute-start.10
  9.2 36.2 %collective-permute-done.8 = bf16[576,1536]{1,0:T(8,128)(2,1)S(1)} collective-permute-done((bf16[576,1536]{1,0:T(8,128)(2,1)S(1)}, bf16[576,1536]{1,0:T(8,128)(2,1)S(1)}, u32[]{:S(2)}, u32[]{:S(2)}) %collective-permute-start.8) | collective-permute-done | bytes 1769504 | tf_op jit(solution)/shard_map/ppermute | solution.py:48
  45.4 37.2 %collective-permute-done.9 = bf16[576,1536]{1,0:T(8,128)(2,1)S(1)} collective-permute-done((bf16[576,1536]{1,0:T(8,128)(2,1)S(1)}, bf16[576,1536]{1,0:T(8,128)(2,1)S(1)}, u32[]{:S(2)}, u32[]{:S(2)}) %collective-permute-start.9) | collective-permute-done | bytes 1769504 | tf_op jit(solution)/shard_map/ppermute | solution.py:48
  82.6 1.5 collective-permute-done.10
  84.2 3.5 %pad_maximum_fusion.refs_1_.refs_4_ = bf16[4,576,1536]{2,1,0:T(8,128)(2,1)} fusion(bf16[1,576,1536]{2,1,0:T(8,128)(2,1)S(1)} %bitcast.190, bf16[1,576,1536]{2,1,0:T(8,128)(2,1)S(1)} %bitcast.189, bf16[1,576,1536]{2,1,0:T(8,128)(2,1)S(1)} %bitcast.188, bf16[1,576,1536]{2,1,0:T(8,128)(2,1)S(1)} %maximum_bitcast_fusion), kind=kLoop, calls=%fused_computation | loop fusion | flops 10616832 | bytes 14155776 | tf_op jit(solution)/shard_map/stack | solution.py:334
  88.5 15.5 %all_to_all.20.in_ref = bf16[16,80,128]{2,1,0:T(8,128)(2,1)S(1)} all-to-all(bf16[16,80,128]{2,1,0:T(8,128)(2,1)S(1)} %shard_map.136), channel_id=1, replica_groups=mesh['seq'=16,'exp'=8] {'seq'}, dimensions={0} | all-to-all | bytes 655360 | tf_op jit(solution)/shard_map/all_to_all | solution.py:148
  104.8 6.0 %all-to-all-start.2 = ((bf16[16,64,128]{2,1,0:T(8,128)(2,1)}), bf16[16,64,128]{2,1,0:T(8,128)(2,1)S(1)}, u32[]{:S(2)}, u32[]{:S(2)}) async-start(bf16[16,64,128]{2,1,0:T(8,128)(2,1)} %shard_map.137), calls=%async_computation.2 | async-start | bytes 524288 | tf_op jit(solution)/shard_map/all_to_all | solution.py:154
  111.0 6.1 %all-to-all-done.2 = bf16[16,64,128]{2,1,0:T(8,128)(2,1)S(1)} async-done(((bf16[16,64,128]{2,1,0:T(8,128)(2,1)}), bf16[16,64,128]{2,1,0:T(8,128)(2,1)S(1)}, u32[]{:S(2)}, u32[]{:S(2)}) %all-to-all-start.2) | async-done | bytes 262176 | tf_op jit(solution)/shard_map/all_to_all | solution.py:154
  117.1 11.8 %shard_map.138 = bf16[2,4,64,1536]{3,2,1,0:T(8,128)(2,1)S(1)} custom-call(s32[14]{0:T(128)S(1)} %stack.117.place.ids, bf16[128,1024]{1,0:T(8,128)(2,1)S(1)} %copy-done.2, bf16[128,1024]{1,0:T(8,128)(2,1)S(1)} %copy-done, bf16[128,1024]{1,0:T(8,128)(2,1)S(1)} %copy-done.1, bf16[128,1024]{1,0:T(8,128)(2,1)S(1)} %copy-done.3, f32[8,128]{1,0:T(8,128)S(1)} %copy-done.4, ...), custom_call_target="tpu_custom_call" | custom-call | tf_op jit(solution)/shard_map/pallas_call | solution.py:159
  130.7 3.4 all-to-all-start
  134.1 1.5 fusion.2
  135.6 2.1 collective-permute-start.1
  139.0 2.2 collective-permute-start.3
  141.3 1.5 dynamic-slice_bitcast_fusion.3
  145.6 4.7 %collective-permute-done.3 = bf16[64,1536]{1,0:T(8,128)(2,1)S(1)} collective-permute-done((bf16[64,1536]{1,0:T(8,128)(2,1)S(1)}, bf16[64,1536]{1,0:T(8,128)(2,1)S(1)}, u32[]{:S(2)}, u32[]{:S(2)}) %collective-permute-start.3) | collective-permute-done | bytes 196640 | tf_op jit(solution)/shard_map/ppermute | solution.py:48
  153.2 3.8 %collective-permute-done.4 = bf16[64,1664]{1,0:T(8,128)(2,1)S(1)} collective-permute-done((bf16[64,1664]{1,0:T(8,128)(2,1)S(1)}, bf16[64,1664]{1,0:T(8,128)(2,1)S(1)}, u32[]{:S(2)}, u32[]{:S(2)}) %collective-permute-start.4) | collective-permute-done | bytes 213024 | tf_op jit(solution)/shard_map/ppermute | solution.py:48
  157.0 1.3 collective-permute-start.6
  159.2 21.2 %collective-permute-start.25 = (bf16[288,1536]{1,0:T(8,128)(2,1)}, bf16[288,1536]{1,0:T(8,128)(2,1)S(1)}, u32[]{:S(2)}, u32[]{:S(2)}) collective-permute-start(bf16[288,1536]{1,0:T(8,128)(2,1)} %get-tuple-element.12), channel_id=1, source_target_pairs={{0,6},{1,7},{2,0},{3,1},{4,2},{5,3},{6,4},{7,5},{8,14},{9,15},{10,... | collective-permute-start | bytes 2654216 | tf_op jit(solution)/shard_map/ppermute | solution.py:48
  181.2 2.7 collective-permute-start.13
  185.2 6.1 %collective-permute-done.25 = bf16[288,1536]{1,0:T(8,128)(2,1)S(1)} collective-permute-done((bf16[288,1536]{1,0:T(8,128)(2,1)}, bf16[288,1536]{1,0:T(8,128)(2,1)S(1)}, u32[]{:S(2)}, u32[]{:S(2)}) %collective-permute-start.25) | collective-permute-done | bytes 884768 | tf_op jit(solution)/shard_map/ppermute | solution.py:48
  191.4 3.5 collective-permute-done.24
  195.7 2.9 collective-permute-start.15
  198.6 2.4 pad_maximum_fusion.1.own_ref
  201.0 9.3 %shard_map.139 = bf16[4,1,64,1280]{3,2,1,0:T(8,128)(2,1)S(1)} custom-call(s32[14]{0:T(128)S(1)} %stack.117.place.ids, bf16[4,64,1664]{2,1,0:T(8,128)(2,1)S(1)} %pad_maximum_fusion.6.refs_0_, bf16[4,576,1536]{2,1,0:T(8,128)(2,1)} %pad_maximum_fusion.refs_1_.refs_4_, bf16[4,576,1536]{2,1,0:T(8,128)(2,1)} %collective-permute-done.11.refs_2_.refs_5_), custom_call_target="tpu_custom_call" | custom-call | tf_op jit(solution)/shard_map/pallas_call | solution.py:219
  210.3 19.1 %shard_map.140 = bf16[4,3,64,1280]{3,2,1,0:T(8,128)(2,1)S(1)} custom-call(s32[14]{0:T(128)S(1)} %stack.117.place.ids, bf16[4,64,1664]{2,1,0:T(8,128)(2,1)S(1)} %collective-permute-done.12.refs_0_, bf16[4,64,1664]{2,1,0:T(8,128)(2,1)S(1)} %collective-permute-done.13.refs_1_, bf16[2,64,1664]{2,1,0:T(8,128)(2,1)S(1)} %collective-permute-done.14.refs_2_, ...), custom_call_target="tpu_custom_call" | custom-call | tf_op jit(solution)/shard_map/pallas_call | solution.py:219
  229.6 5.4 %collective-permute-start.18 = (bf16[2,64,1280]{2,1,0:T(8,128)(2,1)S(1)}, bf16[2,64,1280]{2,1,0:T(8,128)(2,1)S(1)}, u32[]{:S(2)}, u32[]{:S(2)}) collective-permute-start(bf16[2,64,1280]{2,1,0:T(8,128)(2,1)S(1)} %get-tuple-element.31), channel_id=1, source_target_pairs={{0,6},{1,7},{2,0},{3,1},{4,2},{5,3},{6,4},{7,5},{8,14},{9,15},{10,... | collective-permute-start | bytes 983048 | tf_op jit(solution)/shard_map/ppermute | solution.py:48
  235.0 8.3 %collective-permute-done.16 = bf16[2,64,1280]{2,1,0:T(8,128)(2,1)S(1)} collective-permute-done((bf16[2,64,1280]{2,1,0:T(8,128)(2,1)S(1)}, bf16[2,64,1280]{2,1,0:T(8,128)(2,1)S(1)}, u32[]{:S(2)}, u32[]{:S(2)}) %collective-permute-start.16) | collective-permute-done | bytes 327712 | tf_op jit(solution)/shard_map/ppermute | solution.py:48
  244.8 2.2 collective-permute-start.19
  247.0 14.4 %collective-permute-done.17 = bf16[4,64,1280]{2,1,0:T(8,128)(2,1)S(1)} collective-permute-done((bf16[4,64,1280]{2,1,0:T(8,128)(2,1)S(1)}, bf16[4,64,1280]{2,1,0:T(8,128)(2,1)S(1)}, u32[]{:S(2)}, u32[]{:S(2)}) %collective-permute-start.17) | collective-permute-done | bytes 655392 | tf_op jit(solution)/shard_map/ppermute | solution.py:48
  264.8 2.1 collective-permute-start.21
  266.9 8.3 %collective-permute-done.20 = bf16[4,64,768]{2,1,0:T(8,128)(2,1)S(1)} collective-permute-done((bf16[4,64,768]{2,1,0:T(8,128)(2,1)}, bf16[4,64,768]{2,1,0:T(8,128)(2,1)S(1)}, u32[]{:S(2)}, u32[]{:S(2)}) %collective-permute-start.20) | collective-permute-done | bytes 393248 | tf_op jit(solution)/shard_map/ppermute | solution.py:48
  275.4 3.5 collective-permute-start.23
  279.2 3.1 collective-permute-done.22
  283.6 15.6 %shard_map.141 = bf16[4,4,64,1536]{3,2,1,0:T(8,128)(2,1)S(1)} custom-call(s32[14]{0:T(128)S(1)} %stack.117.place.ids, bf16[4,4,64,768]{3,2,1,0:T(8,128)(2,1)S(1)} %pad_maximum_fusion.5.h_ref, bf16[4,384,1536]{2,1,0:T(8,128)(2,1)} %pad_maximum_fusion.1.own_ref, bf16[4,384,1536]{2,1,0:T(8,128)(2,1)} %collective-permute-done.27.swap_ref), custom_call_target="tpu_custom_call" | custom-call | tf_op jit(solution)/shard_map/pallas_call | solution.py:255
  299.4 3.2 collective-permute-start.30
  302.6 5.8 %collective-permute-done.28 = bf16[2,64,1536]{2,1,0:T(8,128)(2,1)S(1)} collective-permute-done((bf16[2,64,1536]{2,1,0:T(8,128)(2,1)S(1)}, bf16[2,64,1536]{2,1,0:T(8,128)(2,1)S(1)}, u32[]{:S(2)}, u32[]{:S(2)}) %collective-permute-start.28) | collective-permute-done | bytes 393248 | tf_op jit(solution)/shard_map/ppermute | solution.py:48
  308.8 3.3 collective-permute-start.31
  312.1 9.8 %collective-permute-done.29 = bf16[4,64,1536]{2,1,0:T(8,128)(2,1)S(1)} collective-permute-done((bf16[4,64,1536]{2,1,0:T(8,128)(2,1)S(1)}, bf16[4,64,1536]{2,1,0:T(8,128)(2,1)S(1)}, u32[]{:S(2)}, u32[]{:S(2)}) %collective-permute-start.29) | collective-permute-done | bytes 786464 | tf_op jit(solution)/shard_map/ppermute | solution.py:48
  322.3 3.3 collective-permute-start.32
  325.6 2.2 collective-permute-done.32
  327.8 2.9 collective-permute-done.34
  330.7 3.3 collective-permute-start.33
  334.1 3.1 collective-permute-done.33
  337.2 2.6 collective-permute-done.35
  339.9 11.2 %all_to_all.21 = bf16[4,16,1536]{2,1,0:T(8,128)(2,1)S(1)} all-to-all(bf16[4,16,1536]{2,1,0:T(8,128)(2,1)S(1)} %bitcast.199), channel_id=1, replica_groups={{0,2,4,6},{1,3,5,7},{8,10,12,14},{9,11,13,15},{16,18,20,22},{17,19,21,2..., dimensions={0} | all-to-all | bytes 393216 | tf_op jit(solution)/shard_map/all_to_all | solution.py:400
  (141 shorter events, 23.3 us)
Async XLA Ops:
  3.6 41.8 %collective-permute-start.8 = (bf16[576,1536]{1,0:T(8,128)(2,1)S(1)}, bf16[576,1536]{1,0:T(8,128)(2,1)S(1)}, u32[]{:S(2)}, u32[]{:S(2)}) collective-permute-start(bf16[576,1536]{1,0:T(8,128)(2,1)S(1)} %pad_maximum_fusion.2), channel_id=1, source_target_pairs={{0,2},{1,3},{2,4},{3,5},{4,6},{5,7},{6,0},{7,1},{8,10},{9,11},{10,... | collective-permute-start | bytes 5308424 | tf_op jit(solution)/shard_map/ppermute | solution.py:48
  5.3 77.3 %collective-permute-start.9 = (bf16[576,1536]{1,0:T(8,128)(2,1)S(1)}, bf16[576,1536]{1,0:T(8,128)(2,1)S(1)}, u32[]{:S(2)}, u32[]{:S(2)}) collective-permute-start(bf16[576,1536]{1,0:T(8,128)(2,1)S(1)} %pad_maximum_fusion.3), channel_id=1, source_target_pairs={{0,6},{1,7},{2,0},{3,1},{4,2},{5,3},{6,4},{7,5},{8,14},{9,15},{10,... | collective-permute-start | bytes 5308424 | tf_op jit(solution)/shard_map/ppermute | solution.py:48
  7.2 76.9 %collective-permute-start.10 = (bf16[576,1536]{1,0:T(8,128)(2,1)S(1)}, bf16[576,1536]{1,0:T(8,128)(2,1)S(1)}, u32[]{:S(2)}, u32[]{:S(2)}) collective-permute-start(bf16[576,1536]{1,0:T(8,128)(2,1)S(1)} %pad_maximum_fusion.4), channel_id=1, source_target_pairs={{0,4},{1,5},{2,6},{3,7},{4,0},{5,1},{6,2},{7,3},{8,12},{9,13},{10,... | collective-permute-start | bytes 5308424 | tf_op jit(solution)/shard_map/ppermute | solution.py:48
  84.2 3.7 %copy-start.1 = (bf16[128,1024]{1,0:T(8,128)(2,1)S(1)}, bf16[128,1024]{1,0:T(8,128)(2,1)}, u32[]{:S(2)}) copy-start(bf16[128,1024]{1,0:T(8,128)(2,1)} %v_ref.3) | copy-start | bytes 786436
  84.2 3.7 %copy-start.4 = (f32[8,128]{1,0:T(8,128)S(1)}, f32[8,128]{1,0:T(8,128)}, u32[]{:S(2)}) copy-start(f32[8,128]{1,0:T(8,128)} %ld_ref.3) | copy-start | bytes 12292
  87.7 23.2 %copy-start.10 = (f32[16,2]{0,1:T(2,128)S(1)}, f32[16,2]{0,1:T(2,128)}, u32[]{:S(2)}) copy-start(f32[16,2]{0,1:T(2,128)} %param.24) | copy-start | bytes 388
  87.7 29.4 %copy-start.2 = (bf16[128,1024]{1,0:T(8,128)(2,1)S(1)}, bf16[128,1024]{1,0:T(8,128)(2,1)}, u32[]{:S(2)}) copy-start(bf16[128,1024]{1,0:T(8,128)(2,1)} %q_ref.1) | copy-start | bytes 786436
  87.7 29.4 %copy-start.3 = (bf16[128,1024]{1,0:T(8,128)(2,1)S(1)}, bf16[128,1024]{1,0:T(8,128)(2,1)}, u32[]{:S(2)}) copy-start(bf16[128,1024]{1,0:T(8,128)(2,1)} %g_ref.1) | copy-start | bytes 786436
  87.7 29.4 %copy-start.5 = (f32[1024]{0:T(1024)S(1)}, f32[1024]{0:T(1024)}, u32[]{:S(2)}) copy-start(f32[1024]{0:T(1024)} %param.20) | copy-start | bytes 12292
  87.7 113.3 %collective-permute-start.11 = (bf16[4,576,1536]{2,1,0:T(8,128)(2,1)}, bf16[4,576,1536]{2,1,0:T(8,128)(2,1)}, u32[]{:S(2)}, u32[]{:S(2)}) collective-permute-start(bf16[4,576,1536]{2,1,0:T(8,128)(2,1)} %pad_maximum_fusion.refs_1_.refs_4_), channel_id=1, source_target_pairs={{0,1},{1,0},{2,3},{3,2},{4,5},{5,4},{6,7},{7,6},{8,9},{9,8},{10,11... | collective-permute-start | bytes 21233672 | tf_op jit(solution)/shard_map/ppermute | solution.py:48
  104.8 12.3 %all-to-all-start.2 = ((bf16[16,64,128]{2,1,0:T(8,128)(2,1)}), bf16[16,64,128]{2,1,0:T(8,128)(2,1)S(1)}, u32[]{:S(2)}, u32[]{:S(2)}) async-start(bf16[16,64,128]{2,1,0:T(8,128)(2,1)} %shard_map.137), calls=%async_computation.2 | async-start | bytes 524288 | tf_op jit(solution)/shard_map/all_to_all | solution.py:154
  117.1 12.6 %copy-start.11 = (s32[16,2]{0,1:T(2,128)S(1)}, s32[16,2]{0,1:T(2,128)}, u32[]{:S(2)}) copy-start(s32[16,2]{0,1:T(2,128)} %param.23) | copy-start | bytes 388
  117.1 12.7 %copy-start.9 = (bf16[16,6144]{1,0:T(8,128)(2,1)S(1)}, bf16[16,6144]{1,0:T(8,128)(2,1)}, u32[]{:S(2)}) copy-start(bf16[16,6144]{1,0:T(8,128)(2,1)} %param.14) | copy-start | bytes 589828
  129.0 5.1 %collective-permute-start = (bf16[4,64,1536]{2,1,0:T(8,128)(2,1)S(1)}, bf16[4,64,1536]{2,1,0:T(8,128)(2,1)}, u32[]{:S(2)}, u32[]{:S(2)}) collective-permute-start(bf16[4,64,1536]{2,1,0:T(8,128)(2,1)S(1)} %slice_bitcast_fusion.1), channel_id=1, source_target_pairs={{0,1},{1,0},{2,3},{3,2},{4,5},{5,4},{6,7},{7,6},{8,9},{9,8},{10,11... | collective-permute-start | bytes 2359304 | tf_op jit(solution)/shard_map/ppermute | solution.py:48
  130.7 14.3 %all-to-all-start = ((bf16[4,16,1664]{2,1,0:T(8,128)(2,1)}), bf16[4,16,1664]{2,1,0:T(8,128)(2,1)S(1)}, u32[]{:S(2)}, u32[]{:S(2)}) async-start(bf16[4,16,1664]{2,1,0:T(8,128)(2,1)} %pad_maximum_fusion.12), calls=%async_computation | async-start | bytes 425984 | tf_op jit(solution)/shard_map/all_to_all | solution.py:354
  134.1 7.2 %copy-start.6 = (bf16[1,288,6144]{2,1,0:T(8,128)(2,1)S(1)}, bf16[1,288,6144]{2,1,0:T(8,128)(2,1)}, u32[]{:S(2)}) copy-start(bf16[1,288,6144]{2,1,0:T(8,128)(2,1)} %param.27) | copy-start | bytes 10616836
  135.6 10.0 %collective-permute-start.1 = (bf16[64,1536]{1,0:T(8,128)(2,1)S(1)}, bf16[64,1536]{1,0:T(8,128)(2,1)S(1)}, u32[]{:S(2)}, u32[]{:S(2)}) collective-permute-start(bf16[64,1536]{1,0:T(8,128)(2,1)S(1)} %get-tuple-element.41), channel_id=1, source_target_pairs={{0,2},{1,3},{2,4},{3,5},{4,6},{5,7},{6,0},{7,1},{8,10},{9,11},{10,... | collective-permute-start | bytes 589832 | tf_op jit(solution)/shard_map/ppermute | solution.py:48
  137.7 7.9 %collective-permute-start.2 = (bf16[64,1536]{1,0:T(8,128)(2,1)S(1)}, bf16[64,1536]{1,0:T(8,128)(2,1)S(1)}, u32[]{:S(2)}, u32[]{:S(2)}) collective-permute-start(bf16[64,1536]{1,0:T(8,128)(2,1)S(1)} %get-tuple-element.43), channel_id=1, source_target_pairs={{0,6},{1,7},{2,0},{3,1},{4,2},{5,3},{6,4},{7,5},{8,14},{9,15},{10,... | collective-permute-start | bytes 589832 | tf_op jit(solution)/shard_map/ppermute | solution.py:48
  139.0 11.3 %collective-permute-start.3 = (bf16[64,1536]{1,0:T(8,128)(2,1)S(1)}, bf16[64,1536]{1,0:T(8,128)(2,1)S(1)}, u32[]{:S(2)}, u32[]{:S(2)}) collective-permute-start(bf16[64,1536]{1,0:T(8,128)(2,1)S(1)} %get-tuple-element.42), channel_id=1, source_target_pairs={{0,4},{1,5},{2,6},{3,7},{4,0},{5,1},{6,2},{7,3},{8,12},{9,13},{10,... | collective-permute-start | bytes 589832 | tf_op jit(solution)/shard_map/ppermute | solution.py:48
  142.8 38.4 %collective-permute-start.26 = (bf16[288,1536]{1,0:T(8,128)(2,1)}, bf16[288,1536]{1,0:T(8,128)(2,1)}, u32[]{:S(2)}, u32[]{:S(2)}) collective-permute-start(bf16[288,1536]{1,0:T(8,128)(2,1)} %get-tuple-element.11), channel_id=1, source_target_pairs={{0,4},{1,5},{2,6},{3,7},{4,0},{5,1},{6,2},{7,3},{8,12},{9,13},{10,... | collective-permute-start | bytes 2654216 | tf_op jit(solution)/shard_map/ppermute | solution.py:48
  151.1 5.9 %collective-permute-start.4 = (bf16[64,1664]{1,0:T(8,128)(2,1)S(1)}, bf16[64,1664]{1,0:T(8,128)(2,1)S(1)}, u32[]{:S(2)}, u32[]{:S(2)}) collective-permute-start(bf16[64,1664]{1,0:T(8,128)(2,1)S(1)} %concatenate.78), channel_id=1, source_target_pairs={{0,8},{1,33},{2,10},{3,35},{4,12},{5,37},{6,14},{7,39},{8,16},{9,4... | collective-permute-start | bytes 638984 | tf_op jit(solution)/shard_map/ppermute | solution.py:48
  152.5 6.3 %collective-permute-start.5 = (bf16[64,1664]{1,0:T(8,128)(2,1)S(1)}, bf16[64,1664]{1,0:T(8,128)(2,1)S(1)}, u32[]{:S(2)}, u32[]{:S(2)}) collective-permute-start(bf16[64,1664]{1,0:T(8,128)(2,1)S(1)} %concatenate.78), channel_id=1, source_target_pairs={{0,24},{1,97},{2,26},{3,99},{4,28},{5,101},{6,30},{7,103},{8,0},{9... | collective-permute-start | bytes 638984 | tf_op jit(solution)/shard_map/ppermute | solution.py:48
  157.0 23.4 %collective-permute-start.6 = (bf16[32,1664]{1,0:T(8,128)(2,1)S(1)}, bf16[32,1664]{1,0:T(8,128)(2,1)S(1)}, u32[]{:S(2)}, u32[]{:S(2)}) collective-permute-start(bf16[32,1664]{1,0:T(8,128)(2,1)S(1)} %slice.310), channel_id=1, source_target_pairs={{0,8},{1,33},{2,10},{3,35},{4,12},{5,37},{6,14},{7,39},{8,16},{9,4... | collective-permute-start | bytes 319496 | tf_op jit(solution)/shard_map/ppermute | solution.py:48
  158.8 21.6 %collective-permute-start.7 = (bf16[32,1664]{1,0:T(8,128)(2,1)S(1)}, bf16[32,1664]{1,0:T(8,128)(2,1)S(1)}, u32[]{:S(2)}, u32[]{:S(2)}) collective-permute-start(bf16[32,1664]{1,0:T(8,128)(2,1)S(1)} %slice.311), channel_id=1, source_target_pairs={{0,24},{1,97},{2,26},{3,99},{4,28},{5,101},{6,30},{7,103},{8,0},{9... | collective-permute-start | bytes 319496 | tf_op jit(solution)/shard_map/ppermute | solution.py:48
  159.2 32.1 %collective-permute-start.25 = (bf16[288,1536]{1,0:T(8,128)(2,1)}, bf16[288,1536]{1,0:T(8,128)(2,1)S(1)}, u32[]{:S(2)}, u32[]{:S(2)}) collective-permute-start(bf16[288,1536]{1,0:T(8,128)(2,1)} %get-tuple-element.12), channel_id=1, source_target_pairs={{0,6},{1,7},{2,0},{3,1},{4,2},{5,3},{6,4},{7,5},{8,14},{9,15},{10,... | collective-permute-start | bytes 2654216 | tf_op jit(solution)/shard_map/ppermute | solution.py:48
  180.4 14.5 %collective-permute-start.24 = (bf16[288,1536]{1,0:T(8,128)(2,1)}, bf16[288,1536]{1,0:T(8,128)(2,1)S(1)}, u32[]{:S(2)}, u32[]{:S(2)}) collective-permute-start(bf16[288,1536]{1,0:T(8,128)(2,1)} %get-tuple-element.10), channel_id=1, source_target_pairs={{0,2},{1,3},{2,4},{3,5},{4,6},{5,7},{6,0},{7,1},{8,10},{9,11},{10,... | collective-permute-start | bytes 2654216 | tf_op jit(solution)/shard_map/ppermute | solution.py:48
  180.6 14.4 %collective-permute-start.12 = (bf16[4,64,1664]{2,1,0:T(8,128)(2,1)S(1)}, bf16[4,64,1664]{2,1,0:T(8,128)(2,1)S(1)}, u32[]{:S(2)}, u32[]{:S(2)}) collective-permute-start(bf16[4,64,1664]{2,1,0:T(8,128)(2,1)S(1)} %pad_maximum_fusion.6.refs_0_), channel_id=1, source_target_pairs={{0,32},{1,9},{2,34},{3,11},{4,36},{5,13},{6,38},{7,15},{8,40},{9,1... | collective-permute-start | bytes 2555912 | tf_op jit(solution)/shard_map/ppermute | solution.py:48
  181.2 14.4 %collective-permute-start.13 = (bf16[4,64,1664]{2,1,0:T(8,128)(2,1)S(1)}, bf16[4,64,1664]{2,1,0:T(8,128)(2,1)S(1)}, u32[]{:S(2)}, u32[]{:S(2)}) collective-permute-start(bf16[4,64,1664]{2,1,0:T(8,128)(2,1)S(1)} %pad_maximum_fusion.6.refs_0_), channel_id=1, source_target_pairs={{0,96},{1,25},{2,98},{3,27},{4,100},{5,29},{6,102},{7,31},{8,104},... | collective-permute-start | bytes 2555912 | tf_op jit(solution)/shard_map/ppermute | solution.py:48
  195.0 15.3 %collective-permute-start.14 = (bf16[2,64,1664]{2,1,0:T(8,128)(2,1)S(1)}, bf16[2,64,1664]{2,1,0:T(8,128)(2,1)S(1)}, u32[]{:S(2)}, u32[]{:S(2)}) collective-permute-start(bf16[2,64,1664]{2,1,0:T(8,128)(2,1)S(1)} %slice.312), channel_id=1, source_target_pairs={{0,32},{1,9},{2,34},{3,11},{4,36},{5,13},{6,38},{7,15},{8,40},{9,1... | collective-permute-start | bytes 1277960 | tf_op jit(solution)/shard_map/ppermute | solution.py:48
  195.7 14.7 %collective-permute-start.15 = (bf16[2,64,1664]{2,1,0:T(8,128)(2,1)S(1)}, bf16[2,64,1664]{2,1,0:T(8,128)(2,1)S(1)}, u32[]{:S(2)}, u32[]{:S(2)}) collective-permute-start(bf16[2,64,1664]{2,1,0:T(8,128)(2,1)S(1)} %slice.313), channel_id=1, source_target_pairs={{0,96},{1,25},{2,98},{3,27},{4,100},{5,29},{6,102},{7,31},{8,104},... | collective-permute-start | bytes 1277960 | tf_op jit(solution)/shard_map/ppermute | solution.py:48
  201.0 82.6 %collective-permute-start.27 = (bf16[4,384,1536]{2,1,0:T(8,128)(2,1)}, bf16[4,384,1536]{2,1,0:T(8,128)(2,1)}, u32[]{:S(2)}, u32[]{:S(2)}) collective-permute-start(bf16[4,384,1536]{2,1,0:T(8,128)(2,1)} %pad_maximum_fusion.1.own_ref), channel_id=1, source_target_pairs={{0,1},{1,0},{2,3},{3,2},{4,5},{5,4},{6,7},{7,6},{8,9},{9,8},{10,11... | collective-permute-start | bytes 14155784 | tf_op jit(solution)/shard_map/ppermute | solution.py:48
  229.5 13.8 %collective-permute-start.16 = (bf16[2,64,1280]{2,1,0:T(8,128)(2,1)S(1)}, bf16[2,64,1280]{2,1,0:T(8,128)(2,1)S(1)}, u32[]{:S(2)}, u32[]{:S(2)}) collective-permute-start(bf16[2,64,1280]{2,1,0:T(8,128)(2,1)S(1)} %get-tuple-element.27), channel_id=1, source_target_pairs={{0,2},{1,3},{2,4},{3,5},{4,6},{5,7},{6,0},{7,1},{8,10},{9,11},{10,... | collective-permute-start | bytes 983048 | tf_op jit(solution)/shard_map/ppermute | solution.py:48
  229.6 13.7 %collective-permute-start.18 = (bf16[2,64,1280]{2,1,0:T(8,128)(2,1)S(1)}, bf16[2,64,1280]{2,1,0:T(8,128)(2,1)S(1)}, u32[]{:S(2)}, u32[]{:S(2)}) collective-permute-start(bf16[2,64,1280]{2,1,0:T(8,128)(2,1)S(1)} %get-tuple-element.31), channel_id=1, source_target_pairs={{0,6},{1,7},{2,0},{3,1},{4,2},{5,3},{6,4},{7,5},{8,14},{9,15},{10,... | collective-permute-start | bytes 983048 | tf_op jit(solution)/shard_map/ppermute | solution.py:48
  243.5 17.8 %collective-permute-start.17 = (bf16[4,64,1280]{2,1,0:T(8,128)(2,1)S(1)}, bf16[4,64,1280]{2,1,0:T(8,128)(2,1)S(1)}, u32[]{:S(2)}, u32[]{:S(2)}) collective-permute-start(bf16[4,64,1280]{2,1,0:T(8,128)(2,1)S(1)} %pad_maximum_fusion.9), channel_id=1, source_target_pairs={{0,2},{1,3},{2,4},{3,5},{4,6},{5,7},{6,0},{7,1},{8,10},{9,11},{10,... | collective-permute-start | bytes 1966088 | tf_op jit(solution)/shard_map/ppermute | solution.py:48
  244.8 16.6 %collective-permute-start.19 = (bf16[4,64,1280]{2,1,0:T(8,128)(2,1)S(1)}, bf16[4,64,1280]{2,1,0:T(8,128)(2,1)S(1)}, u32[]{:S(2)}, u32[]{:S(2)}) collective-permute-start(bf16[4,64,1280]{2,1,0:T(8,128)(2,1)S(1)} %pad_maximum_fusion.10), channel_id=1, source_target_pairs={{0,6},{1,7},{2,0},{3,1},{4,2},{5,3},{6,4},{7,5},{8,14},{9,15},{10,... | collective-permute-start | bytes 1966088 | tf_op jit(solution)/shard_map/ppermute | solution.py:48
  263.7 11.5 %collective-permute-start.20 = (bf16[4,64,768]{2,1,0:T(8,128)(2,1)}, bf16[4,64,768]{2,1,0:T(8,128)(2,1)S(1)}, u32[]{:S(2)}, u32[]{:S(2)}) collective-permute-start(bf16[4,64,768]{2,1,0:T(8,128)(2,1)} %concatenate.92), channel_id=1, source_target_pairs={{0,2},{1,3},{2,4},{3,5},{4,6},{5,7},{6,0},{7,1},{8,10},{9,11},{10,... | collective-permute-start | bytes 1179656 | tf_op jit(solution)/shard_map/ppermute | solution.py:48
  264.8 10.5 %collective-permute-start.21 = (bf16[4,64,768]{2,1,0:T(8,128)(2,1)}, bf16[4,64,768]{2,1,0:T(8,128)(2,1)S(1)}, u32[]{:S(2)}, u32[]{:S(2)}) collective-permute-start(bf16[4,64,768]{2,1,0:T(8,128)(2,1)} %concatenate.92), channel_id=1, source_target_pairs={{0,6},{1,7},{2,0},{3,1},{4,2},{5,3},{6,4},{7,5},{8,14},{9,15},{10,... | collective-permute-start | bytes 1179656 | tf_op jit(solution)/shard_map/ppermute | solution.py:48
  275.2 7.1 %collective-permute-start.22 = (bf16[2,64,768]{2,1,0:T(8,128)(2,1)S(1)}, bf16[2,64,768]{2,1,0:T(8,128)(2,1)}, u32[]{:S(2)}, u32[]{:S(2)}) collective-permute-start(bf16[2,64,768]{2,1,0:T(8,128)(2,1)S(1)} %slice.332), channel_id=1, source_target_pairs={{0,2},{1,3},{2,4},{3,5},{4,6},{5,7},{6,0},{7,1},{8,10},{9,11},{10,... | collective-permute-start | bytes 589832 | tf_op jit(solution)/shard_map/ppermute | solution.py:48
  275.4 6.9 %collective-permute-start.23 = (bf16[2,64,768]{2,1,0:T(8,128)(2,1)S(1)}, bf16[2,64,768]{2,1,0:T(8,128)(2,1)}, u32[]{:S(2)}, u32[]{:S(2)}) collective-permute-start(bf16[2,64,768]{2,1,0:T(8,128)(2,1)S(1)} %slice.333), channel_id=1, source_target_pairs={{0,6},{1,7},{2,0},{3,1},{4,2},{5,3},{6,4},{7,5},{8,14},{9,15},{10,... | collective-permute-start | bytes 589832 | tf_op jit(solution)/shard_map/ppermute | solution.py:48
  279.0 4.4 %copy-start.8 = (bf16[4,64,768]{2,1,0:T(8,128)(2,1)S(1)}, bf16[4,64,768]{2,1,0:T(8,128)(2,1)}, u32[]{:S(2)}) copy-start(bf16[4,64,768]{2,1,0:T(8,128)(2,1)} %copy-done.7) | copy-start | bytes 1179652
  299.3 9.1 %collective-permute-start.28 = (bf16[2,64,1536]{2,1,0:T(8,128)(2,1)S(1)}, bf16[2,64,1536]{2,1,0:T(8,128)(2,1)S(1)}, u32[]{:S(2)}, u32[]{:S(2)}) collective-permute-start(bf16[2,64,1536]{2,1,0:T(8,128)(2,1)S(1)} %get-tuple-element.23), channel_id=1, source_target_pairs={{0,32},{1,9},{2,34},{3,11},{4,36},{5,13},{6,38},{7,15},{8,40},{9,1... | collective-permute-start | bytes 1179656 | tf_op jit(solution)/shard_map/ppermute | solution.py:48
  299.4 9.0 %collective-permute-start.30 = (bf16[2,64,1536]{2,1,0:T(8,128)(2,1)S(1)}, bf16[2,64,1536]{2,1,0:T(8,128)(2,1)S(1)}, u32[]{:S(2)}, u32[]{:S(2)}) collective-permute-start(bf16[2,64,1536]{2,1,0:T(8,128)(2,1)S(1)} %get-tuple-element.24), channel_id=1, source_target_pairs={{0,96},{1,25},{2,98},{3,27},{4,100},{5,29},{6,102},{7,31},{8,104},... | collective-permute-start | bytes 1179656 | tf_op jit(solution)/shard_map/ppermute | solution.py:48
  308.7 13.3 %collective-permute-start.29 = (bf16[4,64,1536]{2,1,0:T(8,128)(2,1)S(1)}, bf16[4,64,1536]{2,1,0:T(8,128)(2,1)S(1)}, u32[]{:S(2)}, u32[]{:S(2)}) collective-permute-start(bf16[4,64,1536]{2,1,0:T(8,128)(2,1)S(1)} %pad_maximum_fusion.7), channel_id=1, source_target_pairs={{0,32},{1,9},{2,34},{3,11},{4,36},{5,13},{6,38},{7,15},{8,40},{9,1... | collective-permute-start | bytes 2359304 | tf_op jit(solution)/shard_map/ppermute | solution.py:48
  308.8 13.1 %collective-permute-start.31 = (bf16[4,64,1536]{2,1,0:T(8,128)(2,1)S(1)}, bf16[4,64,1536]{2,1,0:T(8,128)(2,1)S(1)}, u32[]{:S(2)}, u32[]{:S(2)}) collective-permute-start(bf16[4,64,1536]{2,1,0:T(8,128)(2,1)S(1)} %pad_maximum_fusion.8), channel_id=1, source_target_pairs={{0,96},{1,25},{2,98},{3,27},{4,100},{5,29},{6,102},{7,31},{8,104},... | collective-permute-start | bytes 2359304 | tf_op jit(solution)/shard_map/ppermute | solution.py:48
  322.3 5.5 %collective-permute-start.32 = (bf16[32,1536]{1,0:T(8,128)(2,1)S(1)}, bf16[32,1536]{1,0:T(8,128)(2,1)S(1)}, u32[]{:S(2)}, u32[]{:S(2)}) collective-permute-start(bf16[32,1536]{1,0:T(8,128)(2,1)S(1)} %get-tuple-element.37), channel_id=1, source_target_pairs={{0,8},{1,33},{2,10},{3,35},{4,12},{5,37},{6,14},{7,39},{8,16},{9,4... | collective-permute-start | bytes 294920 | tf_op jit(solution)/shard_map/ppermute | solution.py:48
  325.6 5.1 %collective-permute-start.34 = (bf16[32,1536]{1,0:T(8,128)(2,1)S(1)}, bf16[32,1536]{1,0:T(8,128)(2,1)S(1)}, u32[]{:S(2)}, u32[]{:S(2)}) collective-permute-start(bf16[32,1536]{1,0:T(8,128)(2,1)S(1)} %get-tuple-element.38), channel_id=1, source_target_pairs={{0,24},{1,97},{2,26},{3,99},{4,28},{5,101},{6,30},{7,103},{8,0},{9... | collective-permute-start | bytes 294920 | tf_op jit(solution)/shard_map/ppermute | solution.py:48
  330.7 6.5 %collective-permute-start.33 = (bf16[64,1536]{1,0:T(8,128)(2,1)S(1)}, bf16[64,1536]{1,0:T(8,128)(2,1)S(1)}, u32[]{:S(2)}, u32[]{:S(2)}) collective-permute-start(bf16[64,1536]{1,0:T(8,128)(2,1)S(1)} %pad_maximum_fusion.13), channel_id=1, source_target_pairs={{0,8},{1,33},{2,10},{3,35},{4,12},{5,37},{6,14},{7,39},{8,16},{9,4... | collective-permute-start | bytes 589832 | tf_op jit(solution)/shard_map/ppermute | solution.py:48
  334.0 5.7 %collective-permute-start.35 = (bf16[64,1536]{1,0:T(8,128)(2,1)S(1)}, bf16[64,1536]{1,0:T(8,128)(2,1)S(1)}, u32[]{:S(2)}, u32[]{:S(2)}) collective-permute-start(bf16[64,1536]{1,0:T(8,128)(2,1)S(1)} %pad_maximum_fusion.14), channel_id=1, source_target_pairs={{0,24},{1,97},{2,26},{3,99},{4,28},{5,101},{6,30},{7,103},{8,0},{9... | collective-permute-start | bytes 589832 | tf_op jit(solution)/shard_map/ppermute | solution.py:48
  (2 other events, 7.3 us)
